TPU v7x, 256 devices: a whole 4x4x8 slice. The times are simulated.
256 devices in a mesh: seq: 2 (over core), tp: 4 (over x), req: 32 (over z, y).
Axes of the slice: x: 4, y: 4, z: 8, core: 2. Of those that a mesh axis runs over, the one named last changes fastest.
Arguments:
- cache_pool: bfloat16 [2, 32, 8, 16, 128, 256], P('seq', 'req', 'tp'), may hold values from -6 to 6
- fresh_kv: bfloat16 [32, 8, 256, 256], P('req', 'tp', 'seq'), may hold values from -6.2 to 6.2
- queries: bfloat16 [32, 256, 12288], P('req', 'seq', 'tp'), may hold values from -155 to 155
- stretch_owner: int32 [32, 2], replicated, may hold values from 0 to 48, as said below
- stretch_slot: int32 [32, 2], replicated, may hold values from 0 to 15
- recomp: int32 [32, 2, 1], replicated, may hold values from -1 to 15, as said below
Outputs:
- attended: bfloat16 [32, 256, 12288], P('req', 'seq', 'tp')
- deviation: float32 [32, 256], P('req', 'seq')
Inputs may be any that keep to these rules, and one draw needn't show every extreme that they name: `stretch_owner`: every entry is a multiple of 16; the passage's tile t lies on owner stretch_owner + t, counting owners seq-major over seq and req. `recomp`: the entries of one passage's list that are not -1 differ from each other.
All inputs are finite; a program needn't handle non-finite values.
Results may differ from a plain program's by a relative error of at most 0.0049.
Values may be sent and summed in bfloat16 or wider, within the bound.
A program may use at most 64 MiB of HBM per device.

v0:
```python
import jax
import jax.numpy as jnp
from jax import lax
from jax.sharding import PartitionSpec as P

QH = 96
KVH = 8
HD = 128
TILE = 128
STRETCH = 2048


masked_low = -1e30
key_block = 2048


def split_heads(columns, kv_count, per_group):
    return jnp.transpose(columns.reshape(TILE, kv_count, per_group, HD), (1, 2, 0, 3))


def join_heads(result_block):
    kv_count, per_group, tile_rows, head_size = result_block.shape
    return jnp.transpose(result_block, (2, 0, 1, 3)).reshape(
        tile_rows, kv_count * per_group * head_size
    )


def block_update(state, q_block, key_rows, value_rows, key_pos, q_start):
    row_max, row_sum, accum = state
    scores = jnp.einsum(
        "gqtd,gkd->gqtk", q_block, key_rows, preferred_element_type=jnp.float32
    ) * HD ** (-0.5)
    visible = key_pos[None, :] <= (q_start + jnp.arange(TILE, dtype=jnp.int32))[:, None]
    masked = jnp.where(visible[None, None], scores, masked_low)
    new_max = jnp.maximum(row_max, jnp.max(masked, axis=-1))
    probs = jnp.where(visible[None, None], jnp.exp(masked - new_max[..., None]), 0.0)
    factor = jnp.exp(row_max - new_max)
    new_sum = row_sum * factor + jnp.sum(probs, axis=-1)
    new_accum = accum * factor[..., None] + jnp.einsum(
        "gqtk,gkd->gqtd", probs.astype(jnp.bfloat16), value_rows, preferred_element_type=jnp.float32
    )
    return (new_max, new_sum, new_accum)


def on_device(cache_pool, fresh_kv, queries, stretch_owner, stretch_slot, recomp):
    n_req = lax.axis_size("req")
    seq_index = lax.axis_index("seq")
    req_index = lax.axis_index("req")
    kv_local = cache_pool.shape[2]
    tiles_span = STRETCH // TILE
    own_index = seq_index * n_req + req_index
    owner_dest = jnp.transpose(stretch_owner).reshape(-1)
    slot_dest = jnp.transpose(stretch_slot).reshape(-1)
    serving = (own_index >= owner_dest) & (own_index < owner_dest + tiles_span)
    pool_local = cache_pool[0, 0]
    outgoing = jnp.take(pool_local, slot_dest, axis=1)
    outgoing = jnp.where(serving[None, :, None, None], outgoing, jnp.zeros((), outgoing.dtype))
    arrived = lax.all_to_all(outgoing, ("seq", "req"), split_axis=1, concat_axis=1, tiled=True)
    own_owner = stretch_owner[req_index, seq_index]
    context = lax.dynamic_slice_in_dim(arrived, own_owner, tiles_span, 1)
    entries = recomp[req_index, seq_index]
    n_slots = entries.shape[0]
    matches = entries[:, None] == jnp.arange(tiles_span, dtype=jnp.int32)[None, :]
    present = jnp.any(matches, axis=0)
    slot_of = jnp.sum(
        matches.astype(jnp.int32) * jnp.arange(n_slots, dtype=jnp.int32)[:, None], axis=0
    )
    fresh_tiles = fresh_kv[0].reshape(kv_local, n_slots, TILE, 2 * HD)
    replaced = jnp.take(fresh_tiles, slot_of, axis=1)
    blended = jnp.where(present[None, :, None, None], replaced, context).reshape(
        kv_local, STRETCH, 2 * HD
    )
    is_live = entries >= 0
    tile_pick = jnp.maximum(entries, 0)
    chosen = jnp.take(context, tile_pick, axis=1)
    difference = fresh_tiles.astype(jnp.float32) - chosen.astype(jnp.float32)
    partial_value = jnp.sum(difference * difference, axis=(0, 3))
    summed = lax.psum(partial_value, "tp")
    deviation = summed / (2 * KVH * HD) * is_live[:, None].astype(jnp.float32)
    q_local = queries[0]
    heads_local = q_local.shape[1] // HD
    per_kv = QH // KVH
    half_heads = heads_local // 2
    half_cols = half_heads * HD
    kv_count = max(1, half_heads // per_kv)
    per_group = min(half_heads, per_kv)
    second_cols = q_local[:, half_cols:]
    halves = [
        (q_local[:, :half_cols], seq_index, 0),
        (second_cols, seq_index, half_heads // per_kv),
    ]
    group_specs = []
    initial = []
    for columns, source_dev, kv_first in halves:
        source_entries = recomp[req_index, source_dev]
        q_block = split_heads(columns, kv_count, per_group)
        q_start = source_dev * STRETCH + jnp.maximum(source_entries[0], 0) * TILE
        group_specs.append((q_block, kv_first, q_start, source_entries[0] >= 0))
        initial.append(
            (
                jnp.full((kv_count, per_group, TILE), masked_low, jnp.float32),
                jnp.zeros((kv_count, per_group, TILE), jnp.float32),
                jnp.zeros((kv_count, per_group, TILE, HD), jnp.float32),
            )
        )
    shard_part = lax.all_gather(blended, "seq", axis=1, tiled=True)
    part_rows = shard_part.shape[1]
    n_blocks = part_rows // key_block

    def one_block(block_no, inner):
        key_slab = lax.dynamic_slice_in_dim(shard_part, block_no * key_block, key_block, 1)
        block_first = block_no * key_block
        key_pos = block_first + jnp.arange(key_block, dtype=jnp.int32)
        updated = []
        for group_spec, state in zip(group_specs, inner):
            q_block, kv_first, q_start, slot_live = group_spec
            key_rows = key_slab[kv_first : kv_first + kv_count, :, :HD]
            value_rows = key_slab[kv_first : kv_first + kv_count, :, HD:]
            needed = slot_live & (block_first <= q_start + TILE - 1)
            state = lax.cond(
                needed,
                lambda current: block_update(
                    current, q_block, key_rows, value_rows, key_pos, q_start
                ),
                lambda current: current,
                state,
            )
            updated.append(state)
        return tuple(updated)

    finals = lax.fori_loop(0, n_blocks, one_block, tuple(initial))
    pieces = []
    for group_spec, state in zip(group_specs, finals):
        q_block, kv_first, q_start, slot_live = group_spec
        row_max, row_sum, accum = state
        result_block = accum / jnp.where(slot_live, row_sum, 1.0)[..., None]
        result_block = result_block * slot_live.astype(jnp.float32)
        pieces.append(join_heads(result_block).astype(jnp.bfloat16))
    first_half = jnp.concatenate(pieces[:n_slots], axis=0)
    second_half = jnp.concatenate(pieces[n_slots:], axis=0)
    attended = jnp.concatenate([first_half, second_half], axis=1)[None]
    return (attended, deviation)


def solution(mesh):
    placed = (
        P("seq", "req", "tp", None, None, None),
        P("req", "tp", "seq", None),
        P("req", "seq", "tp"),
        P(),
        P(),
        P(),
    )
    return jax.shard_map(
        on_device,
        mesh=mesh,
        in_specs=placed,
        out_specs=(P("req", "seq", "tp"), P("req", "seq")),
        check_vma=False,
    )
```

profile of v0, /device:TPU:1, one launch (start us, length us, event | category | flops | bytes accessed | tf_op | source)
XLA Modules:
  0.0 307.7 jit_solution(6786813053305428545)
XLA Ops:
  7.2 0.0 copy-start
  7.2 0.9 reshape.274
  8.1 0.8 reshape.273
  8.9 0.7 and_bitcast_fusion
  9.5 0.1 and.47
  9.7 0.0 copy-done
  9.7 5.5 %gather_fusion = bf16[64,2,128,256]{3,2,1,0:T(8,128)(2,1)} fusion(bf16[2,16,128,256]{3,2,1,0:T(8,128)(2,1)S(1)} %bitcast.92, s32[1024]{0:T(1024)S(1)} %pad_clamp_fusion), kind=kCustom, calls=%fused_computation | custom fusion | bytes 16777472 | tf_op jit(solution)/shard_map/jit(_take)/gather | solution.py:56
  15.2 7.6 %select_bitcast_fusion = bf16[2,64,128,256]{3,2,0,1:T(8,128)(2,1)} fusion(bf16[64,2,128,256]{3,2,1,0:T(8,128)(2,1)} %gather_fusion, pred[64]{0:T(512)(128)(4,1)S(1)} %and.47, pred[64]{0:T(512)(128)(4,1)S(1)} %compare_and_fusion), kind=kLoop, calls=%fused_computation.51 | loop fusion | flops 8388608 | bytes 16777344 | tf_op jit(solution)/shard_map/jit(_where)/select_n | solution.py:57
  22.8 13.6 %all-to-all-start = ((bf16[2,64,128,256]{3,2,0,1:T(8,128)(2,1)}), bf16[2,64,128,256]{3,2,0,1:T(8,128)(2,1)}, u32[]{:S(2)}, u32[]{:S(2)}) async-start(bf16[2,64,128,256]{3,2,0,1:T(8,128)(2,1)} %select_bitcast_fusion), calls=%async_computation | async-start | bytes 16777216 | tf_op jit(solution)/shard_map/all_to_all | solution.py:58
  36.4 0.0 all-gather.2.cloned.1.call-start
  36.5 0.0 copy-done.8
  36.5 0.6 dynamic_slice.23
  39.0 0.6 fusion.48
  39.6 0.6 iota_compare_fusion
  40.3 183.8 %all-to-all-done = bf16[2,64,128,256]{3,2,0,1:T(8,128)(2,1)} async-done(((bf16[2,64,128,256]{3,2,0,1:T(8,128)(2,1)}), bf16[2,64,128,256]{3,2,0,1:T(8,128)(2,1)}, u32[]{:S(2)}, u32[]{:S(2)}) %all-to-all-start) | async-done | bytes 8388640 | tf_op jit(solution)/shard_map/all_to_all | solution.py:58
  224.1 1.8 dynamic-slice_select_fusion
  225.9 1.5 copy.11
  227.4 0.0 all-gather.2.cloned.1.call-update
  230.7 0.4 copy.12
  231.1 0.1 fusion.47
  231.2 0.2 copy.14
  231.4 0.2 copy.13
  231.6 1.0 fusion.45
  232.7 8.5 %psum.7 = f32[1,128]{1,0:T(1,128)S(1)} all-reduce(f32[1,128]{1,0:T(1,128)S(1)} %bitcast.104), channel_id=1, replica_groups=mesh['seq'=2,'tp'=4,'req'=32] {'tp'}, use_global_device_ids=true, to_apply=%region_11.12 | all-reduce | flops 128 | bytes 1024 | tf_op jit(solution)/shard_map/psum | solution.py:78
  241.2 0.5 broadcast_multiply_fusion
  241.7 6.6 %all-gather.2.cloned.1.call-done = bf16[2,4096,256]{2,1,0:T(8,128)(2,1)} async-done(((bf16[2,2048,256]{2,1,0:T(8,128)(2,1)}), bf16[2,4096,256]{2,1,0:T(8,128)(2,1)}) %all-gather.2.cloned.1.call-update) | async-done | bytes 4194320 | tf_op jit(solution)/shard_map/all_gather | solution.py:106
  248.3 1.0 broadcast.217.clone
  249.3 1.0 broadcast.217
  250.3 44.1 %while.28 = (s32[]{:T(128)}, f32[1,12,128]{2,1,0:T(8,128)S(1)}, f32[1,12,128]{2,1,0:T(8,128)S(1)}, f32[1,12,128,128]{3,2,1,0:T(8,128)}, f32[1,12,128]{2,1,0:T(8,...) while((s32[]{:T(128)}, f32[1,12,128]{2,1,0:T(8,128)S(1)}, ...), condition=%wide.region_9.10_spmd, body=%wide.region_0.9_spmd.sunk | while | flops 3304336640 | bytes 100633152 | solution.py:131
  250.3 1.7 constant_dynamic-slice_fusion.3
  252.0 10.1 %conditional.4 = ((f32[1,12,128]{2,1,0:T(8,128)S(1)}, f32[1,12,128]{2,1,0:T(8,128)S(1)}, f32[1,12,128,128]{3,2,1,0:T(8,128)})) conditional(s32[]{:T(128)} %convert_element_type.96, (f32[1,12,128]{2,1,0:T(8,128)S(1)}, f32[1,12,128]{2,1,0:T(8,128)S(1)}, f32[1,12,128,128]{3,2,1,0:T(8,128)}) %tuple.80, (s32[2048]{0:T(1024)S(1)}, s32[]{:T(128)}, ...), branch_computations={%region_1.1_spmd, %region_2.4_spmd} | conditional | flops 1652167296 | bytes 48215132 | solution.py:120
  252.0 0.0 copy-start.4
  252.0 0.2 broadcast_compare_fusion
  252.3 2.3 fusion
  254.6 3.7 %fusion.9 = f32[1,12,128,128]{3,2,1,0:T(8,128)S(1)} fusion(f32[12,128,2048]{2,1,0:T(8,128)S(1)} %get-tuple-element.568, f32[12,128]{1,0:T(8,128)S(1)} %bitcast.94, pred[128,2048]{1,0:T(8,128)(4,1)S(1)} %broadcast_compare_fusion, f32[1,12,128,128]{3,2,1,0:T(8,128)S(1)} %copy-done.4, bf16[2,2048,256]{2,1,0:T(8,128)(2,1)S(1)} %get-tuple-element.471, ...), kind=kOutput, calls=%fused_computation.9 | convolution fusion | flops 821428224 | bytes 14958592 | tf_op jit(solution)/shard_map/while/body/eval_jaxpr/cond/branch_1_fun/gqtk,gkd->gqtd/dot_general | solution.py:39
  258.3 0.0 copy-start.5
  258.3 3.8 %fusion.2 = f32[12,128]{1,0:T(8,128)S(1)} fusion(f32[12,128,2048]{2,1,0:T(8,128)S(1)} %get-tuple-element.568, f32[12,128]{1,0:T(8,128)S(1)} %bitcast.95, pred[128,2048]{1,0:T(8,128)(4,1)S(1)} %broadcast_compare_fusion), kind=kLoop, calls=%fused_computation.5 | loop fusion | flops 15727104 | bytes 12857344 | tf_op jit(solution)/shard_map/while/body/eval_jaxpr/cond/branch_1_fun/reduce_sum | solution.py:38
  262.1 10.1 %conditional.5 = ((f32[1,12,128]{2,1,0:T(8,128)S(1)}, f32[1,12,128]{2,1,0:T(8,128)S(1)}, f32[1,12,128,128]{3,2,1,0:T(8,128)})) conditional(s32[]{:T(128)} %convert_element_type.96, (f32[1,12,128]{2,1,0:T(8,128)S(1)}, f32[1,12,128]{2,1,0:T(8,128)S(1)}, f32[1,12,128,128]{3,2,1,0:T(8,128)}) %tuple.82, (s32[2048]{0:T(1024)S(1)}, s32[]{:T(128)}, ...), branch_computations={%region_5.5_spmd, %region_6.8_spmd} | conditional | flops 1652167296 | bytes 48215132 | solution.py:120
  262.2 0.0 copy-start.2
  262.2 0.2 broadcast_compare_fusion.1
  262.4 2.3 fusion.22
  264.8 3.7 %fusion.31 = f32[1,12,128,128]{3,2,1,0:T(8,128)S(1)} fusion(f32[12,128,2048]{2,1,0:T(8,128)S(1)} %get-tuple-element.570, f32[12,128]{1,0:T(8,128)S(1)} %bitcast.96, pred[128,2048]{1,0:T(8,128)(4,1)S(1)} %broadcast_compare_fusion.1, f32[1,12,128,128]{3,2,1,0:T(8,128)S(1)} %copy-done.2, bf16[2,2048,256]{2,1,0:T(8,128)(2,1)S(1)} %get-tuple-element.478, ...), kind=kOutput, calls=%fused_computation.33 | convolution fusion | flops 821428224 | bytes 14958592 | tf_op jit(solution)/shard_map/while/body/eval_jaxpr/cond/branch_1_fun/gqtk,gkd->gqtd/dot_general | solution.py:39
  268.4 3.8 %fusion.24 = f32[12,128]{1,0:T(8,128)S(1)} fusion(f32[12,128,2048]{2,1,0:T(8,128)S(1)} %get-tuple-element.570, f32[12,128]{1,0:T(8,128)S(1)} %bitcast.97, pred[128,2048]{1,0:T(8,128)(4,1)S(1)} %broadcast_compare_fusion.1), kind=kLoop, calls=%fused_computation.29 | loop fusion | flops 15727104 | bytes 12857344 | tf_op jit(solution)/shard_map/while/body/eval_jaxpr/cond/branch_1_fun/reduce_sum | solution.py:38
  272.3 1.7 constant_dynamic-slice_fusion.3
  274.1 10.1 %conditional.4 = ((f32[1,12,128]{2,1,0:T(8,128)S(1)}, f32[1,12,128]{2,1,0:T(8,128)S(1)}, f32[1,12,128,128]{3,2,1,0:T(8,128)})) conditional(s32[]{:T(128)} %convert_element_type.96, (f32[1,12,128]{2,1,0:T(8,128)S(1)}, f32[1,12,128]{2,1,0:T(8,128)S(1)}, f32[1,12,128,128]{3,2,1,0:T(8,128)}) %tuple.80, (s32[2048]{0:T(1024)S(1)}, s32[]{:T(128)}, ...), branch_computations={%region_1.1_spmd, %region_2.4_spmd} | conditional | flops 1652167296 | bytes 48215132 | solution.py:120
  274.1 0.0 copy-start.4
  274.1 0.2 broadcast_compare_fusion
  274.3 2.3 fusion
  276.7 3.7 %fusion.9 = f32[1,12,128,128]{3,2,1,0:T(8,128)S(1)} fusion(f32[12,128,2048]{2,1,0:T(8,128)S(1)} %get-tuple-element.568, f32[12,128]{1,0:T(8,128)S(1)} %bitcast.94, pred[128,2048]{1,0:T(8,128)(4,1)S(1)} %broadcast_compare_fusion, f32[1,12,128,128]{3,2,1,0:T(8,128)S(1)} %copy-done.4, bf16[2,2048,256]{2,1,0:T(8,128)(2,1)S(1)} %get-tuple-element.471, ...), kind=kOutput, calls=%fused_computation.9 | convolution fusion | flops 821428224 | bytes 14958592 | tf_op jit(solution)/shard_map/while/body/eval_jaxpr/cond/branch_1_fun/gqtk,gkd->gqtd/dot_general | solution.py:39
  280.4 0.0 copy-start.5
  280.4 3.8 %fusion.2 = f32[12,128]{1,0:T(8,128)S(1)} fusion(f32[12,128,2048]{2,1,0:T(8,128)S(1)} %get-tuple-element.568, f32[12,128]{1,0:T(8,128)S(1)} %bitcast.95, pred[128,2048]{1,0:T(8,128)(4,1)S(1)} %broadcast_compare_fusion), kind=kLoop, calls=%fused_computation.5 | loop fusion | flops 15727104 | bytes 12857344 | tf_op jit(solution)/shard_map/while/body/eval_jaxpr/cond/branch_1_fun/reduce_sum | solution.py:38
  284.2 10.1 %conditional.5 = ((f32[1,12,128]{2,1,0:T(8,128)S(1)}, f32[1,12,128]{2,1,0:T(8,128)S(1)}, f32[1,12,128,128]{3,2,1,0:T(8,128)})) conditional(s32[]{:T(128)} %convert_element_type.96, (f32[1,12,128]{2,1,0:T(8,128)S(1)}, f32[1,12,128]{2,1,0:T(8,128)S(1)}, f32[1,12,128,128]{3,2,1,0:T(8,128)}) %tuple.82, (s32[2048]{0:T(1024)S(1)}, s32[]{:T(128)}, ...), branch_computations={%region_5.5_spmd, %region_6.8_spmd} | conditional | flops 1652167296 | bytes 48215132 | solution.py:120
  284.2 0.0 copy-start.2
  284.3 0.2 broadcast_compare_fusion.1
  284.5 2.3 fusion.22
  286.8 3.7 %fusion.31 = f32[1,12,128,128]{3,2,1,0:T(8,128)S(1)} fusion(f32[12,128,2048]{2,1,0:T(8,128)S(1)} %get-tuple-element.570, f32[12,128]{1,0:T(8,128)S(1)} %bitcast.96, pred[128,2048]{1,0:T(8,128)(4,1)S(1)} %broadcast_compare_fusion.1, f32[1,12,128,128]{3,2,1,0:T(8,128)S(1)} %copy-done.2, bf16[2,2048,256]{2,1,0:T(8,128)(2,1)S(1)} %get-tuple-element.478, ...), kind=kOutput, calls=%fused_computation.33 | convolution fusion | flops 821428224 | bytes 14958592 | tf_op jit(solution)/shard_map/while/body/eval_jaxpr/cond/branch_1_fun/gqtk,gkd->gqtd/dot_general | solution.py:39
  290.5 3.8 %fusion.24 = f32[12,128]{1,0:T(8,128)S(1)} fusion(f32[12,128,2048]{2,1,0:T(8,128)S(1)} %get-tuple-element.570, f32[12,128]{1,0:T(8,128)S(1)} %bitcast.97, pred[128,2048]{1,0:T(8,128)(4,1)S(1)} %broadcast_compare_fusion.1), kind=kLoop, calls=%fused_computation.29 | loop fusion | flops 15727104 | bytes 12857344 | tf_op jit(solution)/shard_map/while/body/eval_jaxpr/cond/branch_1_fun/reduce_sum | solution.py:38
  294.4 0.0 copy-start.1
  294.4 2.5 copy.16
  296.8 1.4 copy.15
  298.3 1.2 multiply_convert_fusion
  299.5 0.1 multiply_convert_fusion.1
  299.6 0.1 maximum_bitcast_fusion
  299.7 1.2 copy.17
  (44 shorter events, 0.2 us)
Async XLA Ops:
  7.2 2.5 copy-start
  22.8 13.7 %copy-start.8 = (s32[32,2]{0,1:T(2,128)S(1)}, s32[32,2]{0,1:T(2,128)}, u32[]{:S(2)}) copy-start(s32[32,2]{0,1:T(2,128)} %param.15) | copy-start | bytes 772
  22.8 16.2 %copy-start.9 = (s32[32,2,1]{0,2,1:T(1,128)S(1)}, s32[32,2,1]{0,2,1:T(1,128)}, u32[]{:S(2)}) copy-start(s32[32,2,1]{0,2,1:T(1,128)} %param.17) | copy-start | bytes 772
  22.8 201.2 %copy-start.7 = (bf16[1,2,128,256]{3,2,1,0:T(8,128)(2,1)S(1)}, bf16[1,2,128,256]{3,2,1,0:T(8,128)(2,1)}, u32[]{:S(2)}) copy-start(bf16[1,2,128,256]{3,2,1,0:T(8,128)(2,1)} %param.13) | copy-start | bytes 393220
  22.8 207.9 %copy-start.6 = (bf16[1,128,3072]{2,1,0:T(8,128)(2,1)S(1)}, bf16[1,128,3072]{2,1,0:T(8,128)(2,1)}, u32[]{:S(2)}) copy-start(bf16[1,128,3072]{2,1,0:T(8,128)(2,1)} %param.14) | copy-start | bytes 2359300
  22.8 201.2 %all-to-all-start = ((bf16[2,64,128,256]{3,2,0,1:T(8,128)(2,1)}), bf16[2,64,128,256]{3,2,0,1:T(8,128)(2,1)}, u32[]{:S(2)}, u32[]{:S(2)}) async-start(bf16[2,64,128,256]{3,2,0,1:T(8,128)(2,1)} %select_bitcast_fusion), calls=%async_computation | async-start | bytes 16777216 | tf_op jit(solution)/shard_map/all_to_all | solution.py:58
  36.4 211.9 %all-gather.2.cloned.1.call-start = ((), (), s32[]{:S(2)}) async-start(), calls=%async_computation.1 | async-start | bytes 6291456 | tf_op jit(solution)/shard_map/all_gather | solution.py:106
  252.0 2.6 copy-start.4
  258.3 3.8 %copy-start.5 = (f32[1,12,128,128]{3,2,1,0:T(8,128)}, f32[1,12,128,128]{3,2,1,0:T(8,128)S(1)}, u32[]{:S(2)}) copy-start(f32[1,12,128,128]{3,2,1,0:T(8,128)S(1)} %fusion.9) | copy-start | bytes 2359300 | tf_op jit(solution)/shard_map/while/body/eval_jaxpr/cond
  262.2 2.6 copy-start.2
  268.4 3.8 %copy-start.3 = (f32[1,12,128,128]{3,2,1,0:T(8,128)}, f32[1,12,128,128]{3,2,1,0:T(8,128)S(1)}, u32[]{:S(2)}) copy-start(f32[1,12,128,128]{3,2,1,0:T(8,128)S(1)} %fusion.31) | copy-start | bytes 2359300 | tf_op jit(solution)/shard_map/while/body/eval_jaxpr/cond
  274.1 2.6 copy-start.4
  280.4 3.8 %copy-start.5 = (f32[1,12,128,128]{3,2,1,0:T(8,128)}, f32[1,12,128,128]{3,2,1,0:T(8,128)S(1)}, u32[]{:S(2)}) copy-start(f32[1,12,128,128]{3,2,1,0:T(8,128)S(1)} %fusion.9) | copy-start | bytes 2359300 | tf_op jit(solution)/shard_map/while/body/eval_jaxpr/cond
  284.2 2.6 copy-start.2
  290.5 3.8 %copy-start.3 = (f32[1,12,128,128]{3,2,1,0:T(8,128)}, f32[1,12,128,128]{3,2,1,0:T(8,128)S(1)}, u32[]{:S(2)}) copy-start(f32[1,12,128,128]{3,2,1,0:T(8,128)S(1)} %fusion.31) | copy-start | bytes 2359300 | tf_op jit(solution)/shard_map/while/body/eval_jaxpr/cond
  294.4 6.5 %copy-start.1 = (bf16[1,1,2,16,128,256]{5,4,3,2,1,0:T(8,128)(2,1)S(1)}, bf16[1,1,2,16,128,256]{5,4,3,2,1,0:T(8,128)(2,1)}, u32[]{:S(2)}) copy-start(bf16[1,1,2,16,128,256]{5,4,3,2,1,0:T(8,128)(2,1)} %param.12) | copy-start | bytes 6291460
Sparse Core Ops, SparseCore 0:
  227.6 20.6 all-gather.1
where the time goes:
time: 308 us
  waiting for transfers between devices  190 us (62%)
  other arithmetic  30.4 us (10%)
  matrix products  24 us (8%)
  local copies, waits for them, and re-layouts  20.8 us (7%)
  between operations  19.4 us (6%)
  starting transfers between devices  13.6 us (4%)
  blocking collectives  8.47 us (3%)
    all_to_all x1, waiting for transfers between devices, on_device(): lax.all_to_all(outgoing, ('seq', 'req'), split_axis=1, concat_axis=1, til...  184 us
    reduce_sum x4, other arithmetic, block_update(): new_sum = row_sum * factor + jnp.sum(probs, axis=-1)  15.1 us
    dot_general x4, matrix products, block_update(): jnp.einsum('gqtk,gkd->gqtd', probs.astype(jnp.bfloat16), value_rows, pref...  14.7 us
    all_to_all x1, starting transfers between devices, on_device(): lax.all_to_all(outgoing, ('seq', 'req'), split_axis=1, concat_axis=1, til...  13.6 us
    dot_general x4, matrix products, block_update(): jnp.einsum('gqtd,gkd->gqtk', q_block, key_rows, preferred_element_type=jn...  9.33 us
    psum x1, blocking collectives, on_device(): summed = lax.psum(partial_value, 'tp')  8.47 us
    select_n x1, other arithmetic, on_device(): jnp.where(serving[None, :, None, None], outgoing, jnp.zeros((), outgoing....  7.63 us
    all_gather x1, waiting for transfers between devices, on_device(): shard_part = lax.all_gather(blended, 'seq', axis=1, tiled=True)  6.65 us
  transfers between devices with their start and end apart: 2, of which 2 were waited for; matrix products, arithmetic and copies ran while one was open for 1% of the time, Pallas kernels for 0%

commit v1 on v0

v1 whole, which is shorter than its diff:
```python
import functools

import jax
import jax.numpy as jnp
import numpy as np
from jax import lax
from jax.experimental import pallas as pl
from jax.experimental.pallas import tpu as pltpu
from jax.sharding import PartitionSpec as P

KVH = 8
HD = 128
TILE = 128
NT = 16
PER_KV = 12
HCOLS = PER_KV * HD
NZ = 8
NY = 4
MESH = pl.DeviceIdType.MESH
LOG2E = 1.4426950408889634
LEVELS = ((14, 10, 7, 3), (17, 13, 8, 4), (20, 15, 10, 4), (28, 20, 12, 4))


def need_weights():
    weights = np.zeros((4, 2, NZ, NZ, NY, 2), np.int32)
    for hop in range(1, 5):
        for way, sign in ((0, 1), (1, -1)):
            for k in range(NZ):
                for d in range(hop, 5):
                    for y in range(NY):
                        if d < 4 or y % 2 == way:
                            weights[hop - 1, way, k, (k + sign * d) % NZ, y] = 1
    return weights.reshape(4, 2, NZ, NZ * NY * 2)


def tables_kernel(tiles, half, entry, tab):
    me = lax.axis_index("req")
    z, y = me // NY, lax.rem(me, NY)

    def wanted(place, k):
        tile = NY * lax.rem(k, 4) + y
        return jnp.where((half[place] == k // 4) & (tiles[place] > tile), 1, 0)

    def columns(d, way):
        return [q for q in range(2 * NY) if d < 4 or (q // 2) % 2 == way]

    for way, sign in ((0, 1), (1, -1)):
        place = jnp.int32(0)
        for slot in range(32):
            tab[way * 32 + slot] = 0
        for d in (4, 3, 2, 1):
            row = lax.rem(z + sign * d + NZ, NZ)
            for q in columns(d, way):
                tab[way * 32 + place] = entry[row * 8 + q]
                place = place + wanted(row * 8 + q, z)
    for j in range(4):
        counts = []
        for way, sign in ((0, 1), (1, -1)):
            far = (j if way == 0 else 4 - j) if j else 4
            k = lax.rem(z - sign * far + NZ, NZ)
            count = jnp.int32(0)
            for d in range(4, far, -1):
                row = lax.rem(k + sign * d + NZ, NZ)
                for q in columns(d, way):
                    count = count + wanted(row * 8 + q, k)
            counts.append((k, count))
        for q in range(2 * NY):
            here = z * 8 + q
            if j:
                (kf, cf), (kb, cb) = counts
                wf, wb = wanted(here, kf), wanted(here, kb)
                tab[64 + j * 8 + q] = cf * wf + cb * wb
                tab[96 + j * 8 + q] = wb
                counts = [(kf, cf + wf), (kb, cb + wb)]
            else:
                way = (q // 2) % 2
                k, count = counts[way]
                w = wanted(here, k)
                tab[64 + q] = jnp.where(w > 0, count, entry[here])
                tab[96 + q] = w
                counts[way] = (k, count + w)


def comm_kernel(
    caps, chunk, tab, pool, fresh, q, ctx, qx, fx,
    poolbuf, stage, r1, r2, r3, r4, yst,
    zsend, zrecv, ysend, yrecv, xsend, xrecv, lsem,
):
    s = lax.axis_index("seq")
    x = lax.axis_index("tp")
    me = lax.axis_index("req")
    z, y = me // NY, lax.rem(me, NY)
    p1, p2, p3, p4 = caps
    core = (1 - s, x, me)
    zdev = [(s, x, lax.rem(z + 1, NZ) * NY + y), (s, x, lax.rem(z + NZ - 1, NZ) * NY + y)]
    ydev = [(s, x, z * NY + lax.rem(y + dy, NY)) for dy in (1, 2, 3)]

    barrier = pltpu.get_barrier_semaphore()
    for device in [core] + zdev + ydev:
        pl.semaphore_signal(barrier, inc=1, device_id=device, device_id_type=MESH)
    pl.semaphore_wait(barrier, 6)

    other = pl.ds(pl.multiple_of((1 - s) * HCOLS, HCOLS), HCOLS)
    mine = pl.ds(pl.multiple_of(s * HCOLS, HCOLS), HCOLS)
    swaps = [(pool.at[1 - s], poolbuf.at[s]), (q.at[:, other], qx.at[s]), (fresh.at[1 - s], fx.at[s])]
    keeps = [(pool.at[s], poolbuf.at[s]), (q.at[:, mine], qx.at[s]), (fresh.at[s], fx.at[s])]
    swaps = [
        pltpu.make_async_remote_copy(
            src_ref=src, dst_ref=dst, send_sem=xsend.at[i], recv_sem=xrecv.at[i],
            device_id=core, device_id_type=MESH,
        )
        for i, (src, dst) in enumerate(swaps)
    ]
    keeps = [pltpu.make_async_copy(src, dst, lsem.at[i]) for i, (src, dst) in enumerate(keeps)]
    for i in range(3):
        swaps[i].start()
        keeps[i].start()
    keeps[0].wait()
    swaps[0].wait()

    buffers = [
        [(stage.at[0], 0), (r1, 0), (r2, 0), (r3, 0), (r4, 0)],
        [(stage.at[1], 0), (r3, p3), (r2, p2), (r1, p1), (r4, p4)],
    ]

    def zcopy(hop, way, i):
        low = i * chunk
        size = min(chunk, caps[hop - 1] - low)
        src, src_at = buffers[way][hop - 1]
        dst, dst_at = buffers[way][hop]
        return pltpu.make_async_remote_copy(
            src_ref=src.at[pl.ds(src_at + low, size)],
            dst_ref=dst.at[pl.ds(dst_at + low, size)],
            send_sem=zsend.at[hop - 1, way, i],
            recv_sem=zrecv.at[hop - 1, way, i],
            device_id=zdev[way],
            device_id_type=MESH,
        )

    def chunks(hop):
        return -(-caps[hop - 1] // chunk)

    for i in range(chunks(1)):
        for way in range(2):
            for place in range(i * chunk, min((i + 1) * chunk, p1)):
                row = tab[way * 32 + place]
                stage[way, place] = poolbuf[row // NT, lax.rem(row, NT)]
            zcopy(1, way, i).start()

    def ycopy(j, dy):
        tile = NY * lax.rem(z - j + NZ, 4) + y
        return pltpu.make_async_remote_copy(
            src_ref=yst.at[j, dy - 1],
            dst_ref=ctx.at[tile],
            send_sem=ysend.at[j, dy - 1],
            recv_sem=yrecv.at[j, dy - 1],
            device_id=ydev[dy - 1],
            device_id_type=MESH,
        )

    def hand_out(j):
        def picked(column, c):
            at = j * 8 + column * 2 + c
            place, side = tab[64 + at], tab[96 + at]
            if j:
                return (r1, r2, r3)[j - 1][place + side * caps[j - 1]]
            near = jnp.where(side > 0, 0, place)
            far = jnp.where(side > 0, place, 0)
            far = far + lax.rem(column, 2) * p4
            local = poolbuf[near // NT, lax.rem(near, NT)]
            return jnp.where(side > 0, r4[far], local)

        for dy in (2, 1, 3):
            column = lax.rem(y + dy, NY)
            for c in range(2):
                yst[j, dy - 1, c] = picked(column, c)
            ycopy(j, dy).start()
        tile = NY * lax.rem(z - j + NZ, 4) + y
        for c in range(2):
            ctx[tile, c] = picked(y, c)

    for hop in (2, 3, 4):
        for i in range(chunks(hop - 1)):
            for way in range(2):
                zcopy(hop - 1, way, i).wait_recv()
                if i < chunks(hop):
                    zcopy(hop, way, i).start()
        if hop == 3:
            hand_out(2)
        if hop == 4:
            hand_out(1)
            hand_out(3)
    for i in range(chunks(4)):
        for way in range(2):
            zcopy(4, way, i).wait_recv()
    hand_out(0)

    for j in range(4):
        for dy in (1, 2, 3):
            ycopy(j, dy).wait()
    for hop in (1, 2, 3, 4):
        for i in range(chunks(hop)):
            for way in range(2):
                zcopy(hop, way, i).wait_send()
    for i in (1, 2):
        keeps[i].wait()
        swaps[i].wait()


def comm_call(level, tab, pool, fresh, q):
    caps = LEVELS[level]
    chunk = 2 if level < len(LEVELS) - 1 else 4
    p1, p2, p3, p4 = caps
    most = -(-p1 // chunk)
    tile = (TILE, 2 * HD)
    bf = jnp.bfloat16
    anyspace = pl.BlockSpec(memory_space=pl.ANY)
    return pl.pallas_call(
        functools.partial(comm_kernel, caps, chunk),
        out_shape=(
            jax.ShapeDtypeStruct((NT, 2) + tile, bf),
            jax.ShapeDtypeStruct((2, TILE, HCOLS), bf),
            jax.ShapeDtypeStruct((2,) + tile, bf),
        ),
        in_specs=[pl.BlockSpec(memory_space=pltpu.SMEM), anyspace, anyspace, anyspace],
        out_specs=(pl.BlockSpec(memory_space=pltpu.VMEM), anyspace, anyspace),
        scratch_shapes=[
            pltpu.VMEM((2, NT) + tile, bf),
            pltpu.VMEM((2, p1) + tile, bf),
            pltpu.VMEM((p1 + p3,) + tile, bf),
            pltpu.VMEM((2 * p2,) + tile, bf),
            pltpu.VMEM((p3 + p1,) + tile, bf),
            pltpu.VMEM((2 * p4,) + tile, bf),
            pltpu.VMEM((4, 3, 2) + tile, bf),
            pltpu.SemaphoreType.DMA((4, 2, most)),
            pltpu.SemaphoreType.DMA((4, 2, most)),
            pltpu.SemaphoreType.DMA((4, 3)),
            pltpu.SemaphoreType.DMA((4, 3)),
            pltpu.SemaphoreType.DMA((3,)),
            pltpu.SemaphoreType.DMA((3,)),
            pltpu.SemaphoreType.DMA((3,)),
        ],
        compiler_params=pltpu.CompilerParams(
            collective_id=1 + level, has_side_effects=True, vmem_limit_bytes=40 * 2**20
        ),
    )(tab, pool, fresh, q)


def attend_kernel(rec, ctx, qx, fx, out, dev, keys, values):
    scale = HD**-0.5 * LOG2E
    for c in range(2):
        entry = rec[c]
        own = fx[c]

        def blend(t, carry):
            tile = jnp.where(t == entry, own, ctx[t, c])
            rows = pl.ds(pl.multiple_of(t * TILE, TILE), TILE)
            keys[c, rows] = tile[:, :HD]
            values[c, rows, :HD] = jnp.ones((TILE, HD), jnp.bfloat16)
            values[c, rows, HD:] = tile[:, HD:]
            return carry

        lax.fori_loop(0, NT, blend, 0)
        cached = ctx[jnp.maximum(entry, 0), c].astype(jnp.float32)
        gap = own.astype(jnp.float32) - cached
        gap = gap * gap
        gap = jnp.transpose(gap[:, :HD] + gap[:, HD:])
        total = jnp.sum(gap, axis=0, keepdims=True) / (2 * KVH * HD)
        dev[c : c + 1] = jnp.where(entry >= 0, total, 0.0)
    dev[2:8] = jnp.zeros((6, TILE), jnp.float32)

    width = 2 * HD

    def scores(slot, c, block):
        raw = lax.dot_general(
            block, keys[c], (((1,), (1,)), ((), ())), preferred_element_type=jnp.float32
        )
        if slot != c:
            return raw
        last = jnp.maximum(rec[c], 0) * TILE + lax.rem(lax.broadcasted_iota(jnp.int32, raw.shape, 0), TILE)
        at = lax.broadcasted_iota(jnp.int32, raw.shape, 1)
        return jnp.where(at <= last, raw, -1e30)

    for slot in range(2):

        def group(i, carry):
            cols = pl.ds(pl.multiple_of(i * width, width), width)
            pair = qx[slot, :, cols]
            block = jnp.concatenate([pair[:, :HD], pair[:, HD:]], axis=0)
            parts = [scores(slot, c, block) for c in range(slot + 1)]
            top = functools.reduce(jnp.maximum, [jnp.max(p, axis=1, keepdims=True) for p in parts])
            total = jnp.zeros((2 * TILE, 2 * HD), jnp.float32)
            for c in range(slot + 1):
                weights = jnp.exp2((parts[c] - top) * scale).astype(jnp.bfloat16)
                total += jnp.dot(weights, values[c], preferred_element_type=jnp.float32)
            result = total[:, HD:] / total[:, :HD]
            result = jnp.where(rec[slot] >= 0, result, 0.0).astype(jnp.bfloat16)
            out[slot, :, cols] = jnp.concatenate([result[:TILE], result[TILE:]], axis=1)
            return carry

        lax.fori_loop(0, PER_KV // 2, group, 0)


def attend_call(rec, ctx, qx, fx):
    vmem = pl.BlockSpec(memory_space=pltpu.VMEM)
    return pl.pallas_call(
        attend_kernel,
        out_shape=(
            jax.ShapeDtypeStruct((2, TILE, HCOLS), jnp.bfloat16),
            jax.ShapeDtypeStruct((8, TILE), jnp.float32),
        ),
        in_specs=[pl.BlockSpec(memory_space=pltpu.SMEM), vmem, vmem, vmem],
        out_specs=(vmem, vmem),
        scratch_shapes=[
            pltpu.VMEM((2, NT * TILE, HD), jnp.bfloat16),
            pltpu.VMEM((2, NT * TILE, 2 * HD), jnp.bfloat16),
        ],
        compiler_params=pltpu.CompilerParams(vmem_limit_bytes=48 * 2**20),
    )(rec, ctx, qx, fx)


def return_kernel(o, devp, out, dev, gathered, osend, orecv, dsend, drecv, lsem):
    s = lax.axis_index("seq")
    x = lax.axis_index("tp")
    me = lax.axis_index("req")
    peers = [(lax.rem(s + ds, 2), lax.rem(x + dx, 4), me) for ds in range(2) for dx in range(4)][1:]
    barrier = pltpu.get_barrier_semaphore()
    for device in peers:
        pl.semaphore_signal(barrier, inc=1, device_id=device, device_id_type=MESH)
    pl.semaphore_wait(barrier, 7)
    mine = pl.ds(pl.multiple_of(s * HCOLS, HCOLS), HCOLS)
    swap = pltpu.make_async_remote_copy(
        src_ref=o.at[1 - s], dst_ref=out.at[:, mine], send_sem=osend, recv_sem=orecv,
        device_id=(1 - s, x, me), device_id_type=MESH,
    )
    swap.start()
    sends = []
    for i, device in enumerate(peers):
        sends.append(
            pltpu.make_async_remote_copy(
                src_ref=devp, dst_ref=gathered.at[i], send_sem=dsend.at[i], recv_sem=drecv.at[i],
                device_id=device, device_id_type=MESH,
            )
        )
        sends[-1].start()
    keep = pltpu.make_async_copy(o.at[s], out.at[:, mine], lsem)
    keep.start()
    total = devp[...]
    for i in range(7):
        sends[i].wait()
        total = total + gathered[i]
    dev[...] = jnp.where(s == 0, total[0:1], total[1:2])
    keep.wait()
    swap.wait()


def return_call(o, devp):
    vmem = pl.BlockSpec(memory_space=pltpu.VMEM)
    return pl.pallas_call(
        return_kernel,
        out_shape=(
            jax.ShapeDtypeStruct((TILE, 2 * HCOLS), jnp.bfloat16),
            jax.ShapeDtypeStruct((1, TILE), jnp.float32),
        ),
        in_specs=[vmem, vmem],
        out_specs=(vmem, vmem),
        scratch_shapes=[
            pltpu.VMEM((7, 8, TILE), jnp.float32),
            pltpu.SemaphoreType.DMA,
            pltpu.SemaphoreType.DMA,
            pltpu.SemaphoreType.DMA((7,)),
            pltpu.SemaphoreType.DMA((7,)),
            pltpu.SemaphoreType.DMA,
        ],
        compiler_params=pltpu.CompilerParams(
            collective_id=0, has_side_effects=True, vmem_limit_bytes=16 * 2**20
        ),
    )(o, devp)


def on_device(cache_pool, fresh_kv, queries, stretch_owner, stretch_slot, recomp):
    entries = recomp[:, :, 0]
    live = entries >= 0
    reach = jnp.where(live, entries + 1, 0)
    tiles = jnp.stack([jnp.where(live[:, 1], NT, reach[:, 0]), reach[:, 1]], axis=1).reshape(-1)
    half = lax.rem(stretch_owner // NT, 2).reshape(-1)
    entry = ((stretch_owner // (2 * NT)) * NT + stretch_slot).reshape(-1)

    rows = jnp.arange(NZ, dtype=jnp.int32)[:, None]
    wanted = ((half[None] == rows // 4) & (tiles[None] > NY * (rows % 4))).astype(jnp.int32)
    need = jnp.max(jnp.sum(wanted[None, None] * need_weights(), axis=-1), axis=(1, 2))
    level = jnp.int32(0)
    for caps in LEVELS[:-1]:
        level = level + jnp.any(need > np.array(caps, np.int32)).astype(jnp.int32)

    smem = pl.BlockSpec(memory_space=pltpu.SMEM)
    tab = pl.pallas_call(
        tables_kernel,
        out_shape=jax.ShapeDtypeStruct((128,), jnp.int32),
        in_specs=[smem] * 3,
        out_specs=smem,
    )(tiles, half, entry)
    ctx, qx, fx = lax.switch(
        level,
        [functools.partial(comm_call, i) for i in range(len(LEVELS))],
        tab, cache_pool[0, 0], fresh_kv[0], queries[0],
    )
    rec = lax.dynamic_index_in_dim(entries, lax.axis_index("req"), 0, keepdims=False)
    o, devp = attend_call(rec, ctx, qx, fx)
    out, dev = return_call(o, devp)
    return out[None], dev


def solution(mesh):
    placed = (
        P("seq", "req", "tp", None, None, None),
        P("req", "tp", "seq", None),
        P("req", "seq", "tp"),
        P(),
        P(),
        P(),
    )
    return jax.shard_map(
        on_device,
        mesh=mesh,
        in_specs=placed,
        out_specs=(P("req", "seq", "tp"), P("req", "seq")),
        check_vma=False,
    )
```

time: 308 us -> 136 us (0.44)
  waiting for transfers between devices: 190 us -> 0 us
  Pallas kernels: 0 us -> 126 us
  other arithmetic: 30.4 us -> 4.72 us
  matrix products: 24 us -> 0 us
  local copies, waits for them, and re-layouts: 20.8 us -> 2.69 us
  between operations: 19.4 us -> 2.66 us
  starting transfers between devices: 13.6 us -> 0 us
  blocking collectives: 8.47 us -> 0 us
    all_to_all x1 -> x0, waiting for transfers between devices: 184 us -> none  [on_device(): lax.all_to_all(outgoing, ('seq', 'req'), split_axis=1, concat_axis=1, til...]
    pallas_call x0 -> x4, Pallas kernels: none -> 126 us  [the longest x1 87.9 us: comm_call(): pl.pallas_call(functools.partial(comm_kernel, caps, chunk), out_shape=(ja...]
    dot_general x8 -> x0, matrix products: 24 us -> none  [the longest x4 14.7 us: block_update(): jnp.einsum('gqtk,gkd->gqtd', probs.astype(jnp.bfloat16), value_rows, pref...]
    reduce_sum x5 -> x1, other arithmetic: 16.2 us -> 0.97 us  [on_device(): jnp.sum(wanted[None, None] * need_weights(), axis=-1)]
    all_to_all x1 -> x0, starting transfers between devices: 13.6 us -> none  [on_device(): lax.all_to_all(outgoing, ('seq', 'req'), split_axis=1, concat_axis=1, til...]
    select_n x3, other arithmetic: 9.44 us -> 0.02 us  [the longest x1 0.01 us: on_device(): jnp.where(live[:, 1], NT, reach[:, 0])]
    psum x1 -> x0, blocking collectives: 8.47 us -> none  [on_device(): summed = lax.psum(partial_value, 'tp')]
    all_gather x1 -> x0, waiting for transfers between devices: 6.65 us -> none  [on_device(): shard_part = lax.all_gather(blended, 'seq', axis=1, tiled=True)]
  transfers between devices with their start and end apart: 2 -> 0, of which waited for: 2 -> 0; matrix products, arithmetic and copies ran while one was open for 1% -> 0% of each run, Pallas kernels for 0% -> 0%
where the time goes in v1:
time: 136 us
  Pallas kernels  126 us (93%)
  other arithmetic  4.72 us (3%)
  local copies, waits for them, and re-layouts  2.69 us (2%)
  between operations  2.66 us (2%)
    pallas_call x1, Pallas kernels, comm_call(): pl.pallas_call(functools.partial(comm_kernel, caps, chunk), out_shape=(ja...  87.9 us
    pallas_call x1, Pallas kernels, attend_call(): pl.pallas_call(attend_kernel, out_shape=(jax.ShapeDtypeStruct((2, TILE, H...  29.5 us
    pallas_call x1, Pallas kernels, return_call(): pl.pallas_call(return_kernel, out_shape=(jax.ShapeDtypeStruct((TILE, 2 *...  6.51 us

profile of v1, /device:TPU:1, one launch (start us, length us, event | category | flops | bytes accessed | tf_op | source)
XLA Modules:
  0.0 136.2 jit_solution(6285530787158754553)
XLA Ops:
  0.6 0.7 broadcast_add_fusion
  1.3 0.7 broadcast_compare_fusion
  2.0 0.1 copy.19
  2.1 0.1 gt.28.tiles
  2.2 0.0 copy-start.1
  2.2 0.7 multiply_add_fusion
  2.9 0.1 copy.18
  3.0 0.1 eq.21.half
  3.1 0.0 copy-start.2
  3.2 0.1 and_convert_fusion
  3.2 1.0 multiply_reduce_fusion
  4.2 0.2 reduce_max.9
  4.4 1.4 %compare_reduce_fusion = (pred[]{:T(512)}, pred[]{:T(512)}, pred[]{:T(512)}) fusion(s32[4]{0:T(128)S(1)} %reduce_max.9, s32[4]{0:T(128)} %constant.89.clone, s32[4]{0:T(128)} %constant.88.clone, s32[4]{0:T(128)} %constant.87.clone), kind=kLoop, calls=%fused_computation.6 | loop fusion | flops 21 | bytes 67 | tf_op jit(solution)/shard_map/reduce_or | solution.py:394
  7.7 0.1 copy.21
  7.8 0.6 reshape.133.entry
  8.4 0.0 copy-done.1
  8.4 0.0 copy-done.2
  8.4 1.9 %shard_map.113 = s32[128]{0:T(128)S(1)} custom-call(s32[64]{0:T(128)} %copy-done.1, s32[64]{0:T(128)} %copy-done.2, s32[64]{0:T(128)} %reshape.133.entry), custom_call_target="tpu_custom_call" | custom-call | tf_op jit(solution)/shard_map/pallas_call | solution.py:397
  10.3 0.0 copy-start
  10.3 88.2 %conditional.1 = ((bf16[16,2,128,256]{3,2,1,0:T(8,128)(2,1)S(1)}, bf16[2,128,1536]{2,1,0:T(8,128)(2,1)S(1)}, bf16[2,128,256]{2,1,0:T(8,128)(2,1)S(1)})) conditional(s32[]{:T(128)} %clamp.3, (s32[128]{0:T(128)S(1)}, bf16[2,16,128,256]{3,2,1,0:T(8,128)(2,1)}, bf16[2,128,256]{2,1,0:T(8,128)(2,1)}, ...), branch_computations={%region_5.6_spmd, %region_6.7_spmd, %region_7.8_spmd, %region_8.9_... | conditional | bytes 8 | solution.py:403
  10.4 87.9 %branch_1_fun.1 = (bf16[16,2,128,256]{3,2,1,0:T(8,128)(2,1)S(1)}, bf16[2,128,1536]{2,1,0:T(8,128)(2,1)S(1)}, bf16[2,128,256]{2,1,0:T(8,128)(2,1)S(1)}) custom-call(s32[128]{0:T(128)S(1)} %get-tuple-element.36.tab, bf16[2,16,128,256]{3,2,1,0:T(8,128)(2,1)} %get-tuple-element.37.pool, bf16[2,128,256]{2,1,0:T(8,128)(2,1)} %get-tuple-element.38.fresh, ...), custom_call_target="tpu_custom_call" | custom-call | tf_op jit(solution)/shard_map/cond/branch_1_fun/pallas_call | solution.py:218
  98.5 0.0 copy-done
  98.5 0.2 dynamic-slice_reduce_fusion.rec
  98.7 29.5 %shard_map.114 = (bf16[2,128,1536]{2,1,0:T(8,128)(2,1)S(1)}, f32[8,128]{1,0:T(8,128)S(1)}) custom-call(s32[2]{0:T(128)S(1)} %dynamic-slice_reduce_fusion.rec, bf16[16,2,128,256]{3,2,1,0:T(8,128)(2,1)S(1)} %get-tuple-element.57.ctx, bf16[2,128,1536]{2,1,0:T(8,128)(2,1)S(1)} %get-tuple-element.58.qx, bf16[2,128,256]{2,1,0:T(8,128)(2,1)S(1)} %get-tuple-element.59.fx), custom_call_target="tpu_custom_call" | custom-call | tf_op jit(solution)/shard_map/pallas_call | solution.py:306
  128.2 6.5 %shard_map.115 = (bf16[128,3072]{1,0:T(8,128)(2,1)S(1)}, f32[1,128]{1,0:T(1,128)S(1)}) custom-call(bf16[2,128,1536]{2,1,0:T(8,128)(2,1)S(1)} %get-tuple-element.60.o, f32[8,128]{1,0:T(8,128)S(1)} %get-tuple-element.61.devp), custom_call_target="tpu_custom_call" | custom-call | tf_op jit(solution)/shard_map/pallas_call | solution.py:359
  134.8 0.9 copy.40
  135.6 0.5 copy.41
  (4 shorter events, 0.0 us)
Async XLA Ops:
  2.2 6.2 %copy-start.1 = (s32[64]{0:T(128)}, s32[64]{0:T(128)S(1)}, u32[]{:S(2)}) copy-start(s32[64]{0:T(128)S(1)} %gt.28.tiles) | copy-start | bytes 772
  3.1 5.3 %copy-start.2 = (s32[64]{0:T(128)}, s32[64]{0:T(128)S(1)}, u32[]{:S(2)}) copy-start(s32[64]{0:T(128)S(1)} %eq.21.half) | copy-start | bytes 772
  10.3 88.2 %copy-start = (s32[32,2,1]{0,2,1:T(1,128)S(1)}, s32[32,2,1]{0,2,1:T(1,128)}, u32[]{:S(2)}) copy-start(s32[32,2,1]{0,2,1:T(1,128)} %param.19) | copy-start | bytes 772
